TPU v7x, 512 devices: a whole 4x4x16 slice. The times are simulated.
512 devices in a mesh: freq: 8 (over z_lo, core), slab: 64 (over z_hi, x, y).
Axes of the slice: x: 4, y: 4, z: 16 (z_hi: 4, z_lo: 4; z = z_hi * 4 + z_lo), core: 2. Of those that a mesh axis runs over, the one named last changes fastest.
Arguments:
- source: float32 [8, 2, 64, 192, 256], P('freq', None, 'slab'), may hold values from -6 to 6
- labels: int32 [64, 192, 256], P('slab'), may hold values from 0 to 7
- speed_table: float32 [8], replicated, may hold values from 0.97 to 1.03
- atten_table: float32 [8], replicated, may hold values from 0 to 0.03
- offsets: int32 [2], replicated, may hold values from 0 to 128, as said below
Outputs:
- traces: float32 [64, 64, 32, 128], P('freq', 'slab')
Inputs may be any that keep to these rules, and one draw needn't show every extreme that they name: One of the two offsets equals min(160, 128).
All inputs are finite; a program needn't handle non-finite values.
Results may differ from a plain program's by a relative error of at most 0.00012.
Values sent between devices are 32-bit elements; how exact they have to be, the bound alone decides.
A program may use at most 64 MiB of HBM per device.

v0:
```python
import functools
import math

import jax
import jax.numpy as jnp
import numpy as np
from jax import lax
from jax.experimental import pallas as pl
from jax.experimental.pallas import tpu as pltpu
from jax.sharding import PartitionSpec as P

MESH = pl.DeviceIdType.MESH
NX, NY, NZ = 192, 256, 64
FX, FY, NF, TS, NMAT = 32, 128, 8, 64, 8
BASE_BIN, K_UNIT = 4, 0.1
F32, BF16 = jnp.float32, jnp.bfloat16


def dft_tables(count):
    points = np.arange(count)
    angle = (points[:, None] * points[None, :] % count) * (2.0 * math.pi / count)
    return np.cos(angle), np.sin(angle)


def halves(table):
    high = np.asarray(table, np.float32).astype(jnp.bfloat16)
    low = (np.asarray(table, np.float64) - high.astype(np.float64)).astype(jnp.bfloat16)
    return high, low


def constant_tables():
    cos_y, sin_y = dft_tables(NY)
    high, low = halves(np.concatenate([cos_y, sin_y], 1))
    table_y = np.concatenate([high, high, low], 0)
    cos_x, sin_x = dft_tables(NX)
    high, low = halves(np.concatenate([cos_x, sin_x], 0))
    table_x = np.concatenate([high, high, low], 1)
    cos_z, sin_z = dft_tables(NZ)
    high, low = halves(np.concatenate([cos_z, sin_z], 0))
    table_z = np.concatenate([high, high, low], 1)
    angle = np.arange(TS) * (2.0 * math.pi / TS)
    wave = np.stack([np.cos(angle), np.sin(angle)]).astype(np.float32)
    return table_y, table_x, table_z, wave


def split(value):
    high = value.astype(BF16)
    return high, (value - high.astype(F32)).astype(BF16)


def dot(left, right):
    return jnp.dot(left, right, preferred_element_type=F32)


def times_table(value, table):
    high, low = split(value)
    return dot(jnp.concatenate([high, low, high], 1), table)


def table_times(table, value):
    high, low = split(value)
    return dot(table, jnp.concatenate([high, low, high], 0))


def combine_rows(product, rows, width, sign):
    real = product[:rows, :width] - sign * product[rows:, width:]
    imag = product[rows:, :width] + sign * product[:rows, width:]
    return real, imag


def combine_tables(product, rows, width, sign):
    real = product[:rows, :width] - sign * product[rows:, width:]
    imag = product[:rows, width:] + sign * product[rows:, :width]
    return real, imag


def along_y(real, imag, table, sign):
    rows = real.shape[0]
    return combine_rows(
        times_table(jnp.concatenate([real, imag], 0), table), rows, NY, sign
    )


def along_x(real, imag, table, sign):
    width = real.shape[1]
    return combine_tables(
        table_times(table, jnp.concatenate([real, imag], 1)), NX, width, sign
    )


def along_z(real, imag, table, sign):
    width = real.shape[1]
    return combine_tables(
        table_times(table, jnp.concatenate([real, imag], 1)), NZ, width, sign
    )


def put_rows(ref, real, imag):
    for part, value in enumerate((real, imag)):
        for i in range(3):
            for half in range(2):
                ref[pl.ds(4 * i + 2 * part + half, 64, stride=12), :] = value[
                    64 * i : 64 * i + 64, 128 * half : 128 * half + 128
                ]


def get_rows(ref, part, per):
    return jnp.concatenate(
        [
            jnp.concatenate(
                [
                    ref[pl.ds(2 * per * i + per * part + half, 64, stride=6 * per), :]
                    for half in range(per)
                ],
                1,
            )
            for i in range(3)
        ],
        0,
    )


def get_lines(ref, part):
    return jnp.concatenate(
        [
            ref[pl.ds(4 * i + 2 * part + half, 64, stride=12), :]
            for i in range(3)
            for half in range(2)
        ],
        1,
    )


def put_lines(ref, real, imag):
    for part, value in enumerate((real, imag)):
        for i in range(3):
            for half in range(2):
                at = 256 * i + 128 * half
                ref[pl.ds(4 * i + 2 * part + half, 64, stride=12), :] = value[:, at : at + 128]


def folded_square(index, count):
    folded = jnp.where(index <= count // 2, index, index - count)
    wavenum = folded.astype(F32) * (2.0 * math.pi / count)
    return wavenum * wavenum


def role_device(frequency, k):
    return 4 * (frequency % 2) + k // 16, 16 * (frequency // 2) + k % 16


def kernel(
    source, labels, speed, atten, offsets, table_y, table_x, table_z, wave_table, out,
    send1, recv1, send2, recv2, send3, recv3, send4, recv4, tissue, window, windows,
    green, spectrum, pot_buf, field_buf, sel_y, sel_x, send_sem, recv_sem,
):
    f = lax.axis_index("freq")
    s = lax.axis_index("slab")
    freq = 2 * (s // 16) + f // 4
    mine = 16 * (f % 4) + s % 16
    home = freq == f

    barrier = pltpu.get_barrier_semaphore()

    def greet(i, carry):
        pl.semaphore_signal(barrier, inc=1, device_id=(freq, i), device_id_type=MESH)
        return carry

    lax.fori_loop(0, 64, greet, 0)

    def greet_last(i, carry):
        pl.semaphore_signal(barrier, inc=1, device_id=role_device(i, s), device_id_type=MESH)
        return carry

    lax.fori_loop(0, NF, greet_last, 0)

    def remote(src, dst, sem, device):
        return pltpu.make_async_remote_copy(
            src_ref=src,
            dst_ref=dst,
            send_sem=send_sem.at[sem],
            recv_sem=recv_sem.at[sem],
            device_id=device,
            device_id_type=MESH,
        )

    def exchange(src, dst, rows, sem):
        def step(i, carry):
            k = lax.rem(mine + i, 64)
            remote(
                src.at[pl.ds(rows * k, rows)],
                dst.at[pl.ds(rows * mine, rows)],
                sem,
                role_device(freq, k),
            ).start()
            return carry

        lax.fori_loop(1, 64, step, 0)
        own = pl.ds(rows * mine, rows)
        pltpu.make_async_copy(src.at[own], dst.at[own], recv_sem.at[sem]).start()

    def arrived(ref, sem):
        pltpu.make_async_copy(ref, ref, recv_sem.at[sem]).wait()

    def sent(ref, rows, sem):
        part = ref.at[pl.ds(0, rows)]
        pltpu.make_async_copy(part, part, send_sem.at[sem]).wait()

    real, imag = along_y(source[0], source[1], table_y[...], -1.0)
    real, imag = along_x(real, imag, table_x[...], -1.0)
    put_rows(send1, real, imag)
    pl.semaphore_wait(barrier, 64 + NF)

    def scatter(i, carry):
        k = lax.rem(mine + i, 64)
        remote(
            send1.at[pl.ds(12 * k, 12)],
            recv1.at[pl.ds(12 * s, 12)],
            0,
            role_device(f, k),
        ).start()
        return carry

    lax.fori_loop(1, 64, scatter, 0)
    own_send = send1.at[pl.ds(12 * mine, 12)]
    own_recv = recv1.at[pl.ds(12 * s, 12)]

    @pl.when(home)
    def _():
        pltpu.make_async_copy(own_send, own_recv, recv_sem.at[0]).start()

    @pl.when(jnp.logical_not(home))
    def _():
        remote(own_send, own_recv, 0, role_device(f, mine)).start()

    stays = home & (mine == s)

    @pl.when(stays)
    def _():
        pltpu.make_async_copy(labels, tissue, recv_sem.at[1]).start()

    @pl.when(jnp.logical_not(stays))
    def _():
        remote(labels, tissue, 1, role_device(f, s)).start()

    wave = K_UNIT * (BASE_BIN + freq).astype(F32)
    k0sq = wave * wave
    shape = (8, 128)
    pot_real, pot_imag = [], []
    largest = jnp.zeros(shape, F32)
    for m in range(NMAT):
        ratio = jnp.full(shape, wave) / jnp.full(shape, speed[m])
        ratio = ratio * ratio
        damp = jnp.full(shape, atten[m])
        pot_real.append(ratio * (1.0 - damp * damp) - k0sq)
        pot_imag.append(2.0 * ratio * damp)
        largest = jnp.maximum(largest, pot_real[m] * pot_real[m] + pot_imag[m] * pot_imag[m])
    eps = jnp.sqrt(largest) + 0.1 * k0sq
    pot_imag = [value - eps for value in pot_imag]
    eps_row = eps[0:1, 0:1]
    lines = (NZ, NY)
    z_sq = folded_square(lax.broadcasted_iota(jnp.int32, lines, 0), NZ)
    y_sq = folded_square(lax.broadcasted_iota(jnp.int32, lines, 1), NY)
    for i in range(3):
        x_sq = folded_square(jnp.full(lines, 64 * i + mine, jnp.int32), NX)
        shifted = z_sq + x_sq + y_sq - k0sq
        denom = shifted * shifted + eps_row * eps_row
        weight = (1.0 / (NX * NY * NZ)) / denom
        green[0, :, NY * i : NY * (i + 1)] = shifted * weight
        green[1, :, NY * i : NY * (i + 1)] = eps_row * weight

    off_x, off_y = offsets[0], offsets[1]
    pick_y = (
        lax.broadcasted_iota(jnp.int32, (NY, FY), 0)
        == lax.broadcasted_iota(jnp.int32, (NY, FY), 1) + off_y
    ).astype(F32).astype(BF16)
    pick_x = (
        lax.broadcasted_iota(jnp.int32, (FX, NX), 1)
        == lax.broadcasted_iota(jnp.int32, (FX, NX), 0) + off_x
    ).astype(F32).astype(BF16)
    for j, at in enumerate((0, 2 * NY)):
        for part in range(2):
            piece = table_y[at : at + NY, NY * part : NY * (part + 1)]
            sel_y[NY * j : NY * (j + 1), FY * part : FY * (part + 1)] = dot(piece, pick_y).astype(BF16)
    for part in range(2):
        piece = table_x[NX * part : NX * (part + 1), :]
        sel_x[FX * part : FX * (part + 1), :] = dot(pick_x, piece).astype(BF16)

    arrived(recv1, 0)
    real, imag = along_z(get_lines(recv1, 0), get_lines(recv1, 1), table_z[...], -1.0)
    spectrum[0] = real
    spectrum[1] = imag

    def filtered(real, imag):
        green_real, green_imag = green[0], green[1]
        return along_z(
            real * green_real - imag * green_imag,
            real * green_imag + imag * green_real,
            table_z[...],
            1.0,
        )

    real, imag = filtered(real, imag)
    put_lines(send2, real, imag)
    exchange(send2, recv2, 12, 2)

    arrived(tissue, 1)
    plane = (NX, NY)
    ids = tissue[...]
    cell_real = jnp.zeros(plane, F32)
    cell_imag = jnp.zeros(plane, F32)
    for m in range(NMAT):
        matched = ids == m
        cell_real = jnp.where(matched, pot_real[m][0:1, 0:1], cell_real)
        cell_imag = jnp.where(matched, pot_imag[m][0:1, 0:1], cell_imag)
    pot_buf[0] = cell_real
    pot_buf[1] = cell_imag

    arrived(recv2, 2)
    real, imag = along_x(get_rows(recv2, 0, 2), get_rows(recv2, 1, 2), table_x[...], 1.0)
    real, imag = along_y(real, imag, table_y[...], 1.0)
    cell_real, cell_imag = pot_buf[0], pot_buf[1]
    inv_eps = 1.0 / eps_row
    gamma_real, gamma_imag = -cell_imag * inv_eps, cell_real * inv_eps
    field_real = gamma_real * real - gamma_imag * imag
    field_imag = gamma_real * imag + gamma_imag * real
    field_buf[0] = field_real
    field_buf[1] = field_imag
    work_real = cell_real * field_real - cell_imag * field_imag
    work_imag = cell_real * field_imag + cell_imag * field_real
    real, imag = along_y(work_real, work_imag, table_y[...], -1.0)
    real, imag = along_x(real, imag, table_x[...], -1.0)
    put_rows(send3, real, imag)
    exchange(send3, recv3, 12, 3)

    def focal(high_mid_low):
        total = None
        for piece in high_mid_low:
            picked = dot(dot(pick_x, piece).astype(BF16), pick_y)
            total = picked if total is None else total + picked
        return total

    def thirds(value):
        high, rest = split(value)
        low = (value - high.astype(F32) - rest.astype(F32)).astype(BF16)
        return high, rest, low

    focal_ids = focal([tissue[...].astype(F32).astype(BF16)])
    focal_real = focal(thirds(field_buf[0]))
    focal_imag = focal(thirds(field_buf[1]))
    cell_real = jnp.zeros((FX, FY), F32)
    cell_imag = jnp.zeros((FX, FY), F32)
    for m in range(NMAT):
        matched = focal_ids == float(m)
        cell_real = jnp.where(matched, pot_real[m][0:1, 0:1], cell_real)
        cell_imag = jnp.where(matched, pot_imag[m][0:1, 0:1], cell_imag)
    gamma_real, gamma_imag = -cell_imag * inv_eps, cell_real * inv_eps

    arrived(recv3, 3)
    real, imag = along_z(get_lines(recv3, 0), get_lines(recv3, 1), table_z[...], -1.0)
    real, imag = filtered(real + spectrum[0], imag + spectrum[1])
    stacked = jnp.concatenate(
        [value[:, NY * i : NY * (i + 1)] for value in (real, imag) for i in range(3)], 0
    )
    high, low = split(stacked)
    product = dot(jnp.concatenate([high, low], 1), jnp.concatenate([sel_y[:NY], sel_y[:NY]], 0)) + dot(
        high, sel_y[NY:]
    )
    real, imag = combine_rows(product, 3 * NZ, FY, 1.0)
    for part, value in enumerate((real, imag)):
        for i in range(3):
            send4[pl.ds(2 * i + part, 64, stride=6), :] = value[64 * i : 64 * i + 64]
    exchange(send4, recv4, 6, 4)
    arrived(recv4, 4)
    product = table_times(
        sel_x[...], jnp.concatenate([get_rows(recv4, 0, 1), get_rows(recv4, 1, 1)], 1)
    )
    real, imag = combine_tables(product, FX, FY, 1.0)
    diff_real = focal_real - real
    diff_imag = focal_imag - imag
    window[:FX] = focal_real - (gamma_real * diff_real - gamma_imag * diff_imag)
    window[FX:] = focal_imag - (gamma_real * diff_imag + gamma_imag * diff_real)

    here = mine == s

    def hand_out(i, carry):
        target = lax.rem(f + i, NF)

        @pl.when(here & (i == 0))
        def _():
            pltpu.make_async_copy(window, windows.at[freq], recv_sem.at[5]).start()

        @pl.when(jnp.logical_not(here & (i == 0)))
        def _():
            remote(window, windows.at[freq], 5, (target, mine)).start()

        return carry

    lax.fori_loop(0, NF, hand_out, 0)
    arrived(windows, 5)
    for t in range(8):
        total = jnp.zeros((FX, FY), F32)
        for j in range(NF):
            phase = (8 * f + t) * (BASE_BIN + j) % TS
            total = total + wave_table[0, phase] * windows[j, :FX] - wave_table[1, phase] * windows[j, FX:]
        out[t, 0] = total

    @pl.when(home)
    def _():
        sent(send1, 12 * 63, 0)

    @pl.when(jnp.logical_not(home))
    def _():
        sent(send1, 12 * 64, 0)

    @pl.when(jnp.logical_not(stays))
    def _():
        pltpu.make_async_copy(labels, labels, send_sem.at[1]).wait()

    sent(send2, 12 * 63, 2)
    sent(send3, 12 * 63, 3)
    sent(send4, 6 * 63, 4)

    @pl.when(here)
    def _():
        part = windows.at[pl.ds(0, NF - 1)]
        pltpu.make_async_copy(part, part, send_sem.at[5]).wait()

    @pl.when(jnp.logical_not(here))
    def _():
        pltpu.make_async_copy(windows, windows, send_sem.at[5]).wait()


def solution(mesh):
    table_y, table_x, table_z, wave_table = constant_tables()
    vmem = pl.BlockSpec(memory_space=pltpu.VMEM)
    smem = pl.BlockSpec(memory_space=pltpu.SMEM)

    def local(source, labels, speed_table, atten_table, offsets):
        chunks = pltpu.VMEM((64 * 12, 128), F32)
        small = pltpu.VMEM((64 * 6, 128), F32)
        return pl.pallas_call(
            kernel,
            out_shape=jax.ShapeDtypeStruct((TS // NF, 1, FX, FY), F32),
            in_specs=[vmem, vmem, smem, smem, smem, vmem, vmem, vmem, smem],
            out_specs=vmem,
            scratch_shapes=[
                chunks, chunks, chunks, chunks, chunks, chunks, small, small,
                pltpu.VMEM((NX, NY), jnp.int32),
                pltpu.VMEM((2 * FX, FY), F32),
                pltpu.VMEM((NF, 2 * FX, FY), F32),
                pltpu.VMEM((2, NZ, 3 * NY), F32),
                pltpu.VMEM((2, NZ, 3 * NY), F32),
                pltpu.VMEM((2, NX, NY), F32),
                pltpu.VMEM((2, NX, NY), F32),
                pltpu.VMEM((2 * NY, 2 * FY), BF16),
                pltpu.VMEM((2 * FX, 3 * NX), BF16),
                pltpu.SemaphoreType.DMA((6,)),
                pltpu.SemaphoreType.DMA((6,)),
            ],
            compiler_params=pltpu.CompilerParams(
                collective_id=0, has_side_effects=True, vmem_limit_bytes=40 * 1024 * 1024
            ),
        )(
            source[0, :, 0], labels[0], speed_table, atten_table, offsets,
            jnp.asarray(table_y), jnp.asarray(table_x), jnp.asarray(table_z), jnp.asarray(wave_table),
        )

    return jax.shard_map(
        local,
        mesh=mesh,
        in_specs=(P("freq", None, "slab", None, None), P("slab", None, None), P(), P(), P()),
        out_specs=P("freq", "slab", None, None),
        check_vma=False,
    )
```

profile of v0, /device:TPU:1, one launch (start us, length us, event | category | flops | bytes accessed | tf_op | source)
XLA Modules:
  0.0 101.7 jit_solution(3114418854535996635)
XLA Ops:
  0.0 0.0 copy-start.7
  0.0 0.0 copy-start.8
  0.0 0.0 copy-start.5
  0.0 0.0 copy-start.6
  0.0 0.6 copy-done.7
  0.7 0.0 copy-done.8
  0.7 0.0 copy-done.5
  0.7 0.0 copy-done.6
  0.7 0.0 copy-start
  0.7 1.1 %copy-done = bf16[768,512]{1,0:T(8,128)(2,1)S(1)} copy-done((bf16[768,512]{1,0:T(8,128)(2,1)S(1)}, bf16[768,512]{1,0:T(8,128)(2,1)}, u32[]{:S(2)}) %copy-start) | copy-done | bytes 786456
  1.8 0.0 copy-start.1
  1.9 1.0 %copy-done.1 = bf16[384,576]{1,0:T(8,128)(2,1)S(1)} copy-done((bf16[384,576]{1,0:T(8,128)(2,1)S(1)}, bf16[384,576]{1,0:T(8,128)(2,1)}, u32[]{:S(2)}) %copy-start.1) | copy-done | bytes 442392
  2.9 0.0 copy-start.2
  2.9 1.0 copy-done.2
  3.9 0.0 copy-start.3
  3.9 0.9 copy-done.3
  4.8 0.0 copy-start.4
  4.8 0.8 copy-done.4
  5.6 95.4 %shard_map.91 = f32[8,1,32,128]{3,2,1,0:T(8,128)S(1)} custom-call(f32[2,192,256]{2,1,0:T(8,128)S(1)} %bitcast.2, s32[192,256]{1,0:T(8,128)S(1)} %bitcast.3, f32[8]{0:T(128)S(1)} %copy-done.6, f32[8]{0:T(128)S(1)} %copy-done.7, s32[2]{0:T(128)S(1)} %copy-done.8, bf16[768,512]{1,0:T(8,128)(2,1)S(1)} %copy-done, bf16[384,576]{1,0:T(8,128)(2,1)S(1)} %copy-done.1, ...), custom_call_target="tpu_custom_call" | custom-call | tf_op jit(solution)/shard_map/pallas_call | solution.py:442
  101.1 0.7 copy.11
Async XLA Ops:
  0.0 0.7 copy-start.7
  0.0 0.7 copy-start.8
  0.0 0.7 copy-start.5
  0.0 0.7 copy-start.6
  0.7 1.1 %copy-start = (bf16[768,512]{1,0:T(8,128)(2,1)S(1)}, bf16[768,512]{1,0:T(8,128)(2,1)}, u32[]{:S(2)}) copy-start(bf16[768,512]{1,0:T(8,128)(2,1)} %constant.8.clone.table_y) | copy-start | bytes 2359300
  1.8 1.0 %copy-start.1 = (bf16[384,576]{1,0:T(8,128)(2,1)S(1)}, bf16[384,576]{1,0:T(8,128)(2,1)}, u32[]{:S(2)}) copy-start(bf16[384,576]{1,0:T(8,128)(2,1)} %constant.9.clone.table_x) | copy-start | bytes 1327108
  2.9 1.0 copy-start.2
  3.9 0.9 copy-start.3
  4.8 0.8 copy-start.4
where the time goes:
time: 102 us
  Pallas kernels  95.4 us (94%)
  local copies, waits for them, and re-layouts  6.28 us (6%)
    pallas_call x1, Pallas kernels, local(): pl.pallas_call(kernel, out_shape=jax.ShapeDtypeStruct((TS // NF, 1, FX, F...  95.4 us
    unnamed x19, local copies, waits for them, and re-layouts  6.28 us

commit v1 on v0

--- a/solution.py
+++ b/solution.py
@@ -146,19 +146,31 @@
 
 
 def role_device(frequency, k):
-    return 4 * (frequency % 2) + k // 16, 16 * (frequency // 2) + k % 16
+    block = frequency // 2 + 4 * (frequency % 2)
+    return 4 * (block % 2) + k // 16, 16 * (block // 2) + k % 16
 
 
 def kernel(
-    source, labels, speed, atten, offsets, table_y, table_x, table_z, wave_table, out,
+    source_in, labels, speed, atten, offsets, table_y_in, table_x_in, table_z_in, wave_table, out,
+    source, table_y, table_x, table_z,
     send1, recv1, send2, recv2, send3, recv3, send4, recv4, tissue, window, windows,
-    green, spectrum, pot_buf, field_buf, sel_y, sel_x, send_sem, recv_sem,
+    green, spectrum, field_buf, sel_y, sel_x, load_sem, send_sem, recv_sem, pass_sem, relay_sem,
 ):
     f = lax.axis_index("freq")
     s = lax.axis_index("slab")
-    freq = 2 * (s // 16) + f // 4
+    block = 2 * (s // 16) + f // 4
+    freq = 2 * (block % 4) + block // 4
     mine = 16 * (f % 4) + s % 16
     home = freq == f
+
+    loads = [
+        pltpu.make_async_copy(src, dst, load_sem.at[i])
+        for i, (src, dst) in enumerate(
+            ((source_in, source), (table_y_in, table_y), (table_x_in, table_x), (table_z_in, table_z))
+        )
+    ]
+    for load in loads:
+        load.start()
 
     barrier = pltpu.get_barrier_semaphore()
 
@@ -168,11 +180,9 @@
 
     lax.fori_loop(0, 64, greet, 0)
 
-    def greet_last(i, carry):
-        pl.semaphore_signal(barrier, inc=1, device_id=role_device(i, s), device_id_type=MESH)
-        return carry
-
-    lax.fori_loop(0, NF, greet_last, 0)
+    for step in range(1, NF):
+        near = lax.rem(f + step, NF)
+        pl.semaphore_signal(barrier, inc=1, device_id=(near, s), device_id_type=MESH)
 
     def remote(src, dst, sem, device):
         return pltpu.make_async_remote_copy(
@@ -206,10 +216,13 @@
         part = ref.at[pl.ds(0, rows)]
         pltpu.make_async_copy(part, part, send_sem.at[sem]).wait()
 
+    loads[0].wait()
+    loads[1].wait()
     real, imag = along_y(source[0], source[1], table_y[...], -1.0)
+    loads[2].wait()
     real, imag = along_x(real, imag, table_x[...], -1.0)
     put_rows(send1, real, imag)
-    pl.semaphore_wait(barrier, 64 + NF)
+    pl.semaphore_wait(barrier, 64 + NF - 1)
 
     def scatter(i, carry):
         k = lax.rem(mine + i, 64)
@@ -234,14 +247,6 @@
         remote(own_send, own_recv, 0, role_device(f, mine)).start()
 
     stays = home & (mine == s)
-
-    @pl.when(stays)
-    def _():
-        pltpu.make_async_copy(labels, tissue, recv_sem.at[1]).start()
-
-    @pl.when(jnp.logical_not(stays))
-    def _():
-        remote(labels, tissue, 1, role_device(f, s)).start()
 
     wave = K_UNIT * (BASE_BIN + freq).astype(F32)
     k0sq = wave * wave
@@ -286,6 +291,23 @@
         piece = table_x[NX * part : NX * (part + 1), :]
         sel_x[FX * part : FX * (part + 1), :] = dot(pick_x, piece).astype(BF16)
 
+    loads[3].wait()
+    @pl.when(home)
+    def _():
+        sent(send1, 12 * 63, 0)
+
+    @pl.when(jnp.logical_not(home))
+    def _():
+        sent(send1, 12 * 64, 0)
+
+    @pl.when(stays)
+    def _():
+        pltpu.make_async_copy(labels, tissue, recv_sem.at[1]).start()
+
+    @pl.when(jnp.logical_not(stays))
+    def _():
+        remote(labels, tissue, 1, role_device(f, s)).start()
+
     arrived(recv1, 0)
     real, imag = along_z(get_lines(recv1, 0), get_lines(recv1, 1), table_z[...], -1.0)
     spectrum[0] = real
@@ -304,6 +326,9 @@
     put_lines(send2, real, imag)
     exchange(send2, recv2, 12, 2)
 
+    arrived(recv2, 2)
+    real, imag = along_x(get_rows(recv2, 0, 2), get_rows(recv2, 1, 2), table_x[...], 1.0)
+    real, imag = along_y(real, imag, table_y[...], 1.0)
     arrived(tissue, 1)
     plane = (NX, NY)
     ids = tissue[...]
@@ -313,13 +338,6 @@
         matched = ids == m
         cell_real = jnp.where(matched, pot_real[m][0:1, 0:1], cell_real)
         cell_imag = jnp.where(matched, pot_imag[m][0:1, 0:1], cell_imag)
-    pot_buf[0] = cell_real
-    pot_buf[1] = cell_imag
-
-    arrived(recv2, 2)
-    real, imag = along_x(get_rows(recv2, 0, 2), get_rows(recv2, 1, 2), table_x[...], 1.0)
-    real, imag = along_y(real, imag, table_y[...], 1.0)
-    cell_real, cell_imag = pot_buf[0], pot_buf[1]
     inv_eps = 1.0 / eps_row
     gamma_real, gamma_imag = -cell_imag * inv_eps, cell_real * inv_eps
     field_real = gamma_real * real - gamma_imag * imag
@@ -381,23 +399,49 @@
     window[:FX] = focal_real - (gamma_real * diff_real - gamma_imag * diff_imag)
     window[FX:] = focal_imag - (gamma_real * diff_imag + gamma_imag * diff_real)
 
-    here = mine == s
-
-    def hand_out(i, carry):
-        target = lax.rem(f + i, NF)
-
-        @pl.when(here & (i == 0))
-        def _():
-            pltpu.make_async_copy(window, windows.at[freq], recv_sem.at[5]).start()
-
-        @pl.when(jnp.logical_not(here & (i == 0)))
-        def _():
-            remote(window, windows.at[freq], 5, (target, mine)).start()
-
-        return carry
-
-    lax.fori_loop(0, NF, hand_out, 0)
-    arrived(windows, 5)
+    at_home = (mine == s) & (freq % 2 == f % 2)
+
+    def window_copy(target):
+        return pltpu.make_async_remote_copy(
+            src_ref=window,
+            dst_ref=windows.at[freq],
+            send_sem=send_sem.at[5],
+            recv_sem=pass_sem.at[freq],
+            device_id=(target, mine),
+            device_id_type=MESH,
+        )
+
+    for step in range(4):
+        target = 2 * lax.rem(f // 2 + step, 4) + freq % 2
+        if step:
+            window_copy(target).start()
+        else:
+
+            @pl.when(at_home)
+            def _():
+                pltpu.make_async_copy(window, windows.at[freq], pass_sem.at[freq]).start()
+
+            @pl.when(jnp.logical_not(at_home))
+            def _():
+                window_copy(target).start()
+
+    def landed(j):
+        pltpu.make_async_copy(windows.at[j], windows.at[j], pass_sem.at[j]).wait()
+
+    sibling = f + 1 - 2 * (f % 2)
+    for step in range(4):
+        j = 2 * lax.rem(f // 2 + step, 4) + f % 2
+        landed(j)
+        pltpu.make_async_remote_copy(
+            src_ref=windows.at[j],
+            dst_ref=windows.at[j],
+            send_sem=relay_sem,
+            recv_sem=pass_sem.at[j],
+            device_id=(sibling, s),
+            device_id_type=MESH,
+        ).start()
+    for step in range(4):
+        landed(2 * step + 1 - f % 2)
     for t in range(8):
         total = jnp.zeros((FX, FY), F32)
         for j in range(NF):
@@ -405,14 +449,6 @@
             total = total + wave_table[0, phase] * windows[j, :FX] - wave_table[1, phase] * windows[j, FX:]
         out[t, 0] = total
 
-    @pl.when(home)
-    def _():
-        sent(send1, 12 * 63, 0)
-
-    @pl.when(jnp.logical_not(home))
-    def _():
-        sent(send1, 12 * 64, 0)
-
     @pl.when(jnp.logical_not(stays))
     def _():
         pltpu.make_async_copy(labels, labels, send_sem.at[1]).wait()
@@ -421,19 +457,24 @@
     sent(send3, 12 * 63, 3)
     sent(send4, 6 * 63, 4)
 
-    @pl.when(here)
-    def _():
-        part = windows.at[pl.ds(0, NF - 1)]
+    @pl.when(at_home)
+    def _():
+        part = windows.at[pl.ds(0, 3)]
         pltpu.make_async_copy(part, part, send_sem.at[5]).wait()
 
-    @pl.when(jnp.logical_not(here))
-    def _():
-        pltpu.make_async_copy(windows, windows, send_sem.at[5]).wait()
+    @pl.when(jnp.logical_not(at_home))
+    def _():
+        part = windows.at[pl.ds(0, 4)]
+        pltpu.make_async_copy(part, part, send_sem.at[5]).wait()
+
+    relayed = windows.at[pl.ds(0, 4)]
+    pltpu.make_async_copy(relayed, relayed, relay_sem).wait()
 
 
 def solution(mesh):
     table_y, table_x, table_z, wave_table = constant_tables()
     vmem = pl.BlockSpec(memory_space=pltpu.VMEM)
+    hbm = pl.BlockSpec(memory_space=pltpu.HBM)
     smem = pl.BlockSpec(memory_space=pltpu.SMEM)
 
     def local(source, labels, speed_table, atten_table, offsets):
@@ -442,9 +483,13 @@
         return pl.pallas_call(
             kernel,
             out_shape=jax.ShapeDtypeStruct((TS // NF, 1, FX, FY), F32),
-            in_specs=[vmem, vmem, smem, smem, smem, vmem, vmem, vmem, smem],
+            in_specs=[hbm, hbm, smem, smem, smem, hbm, hbm, hbm, smem],
             out_specs=vmem,
             scratch_shapes=[
+                pltpu.VMEM((2, NX, NY), F32),
+                pltpu.VMEM(table_y.shape, BF16),
+                pltpu.VMEM(table_x.shape, BF16),
+                pltpu.VMEM(table_z.shape, BF16),
                 chunks, chunks, chunks, chunks, chunks, chunks, small, small,
                 pltpu.VMEM((NX, NY), jnp.int32),
                 pltpu.VMEM((2 * FX, FY), F32),
@@ -452,14 +497,16 @@
                 pltpu.VMEM((2, NZ, 3 * NY), F32),
                 pltpu.VMEM((2, NZ, 3 * NY), F32),
                 pltpu.VMEM((2, NX, NY), F32),
-                pltpu.VMEM((2, NX, NY), F32),
                 pltpu.VMEM((2 * NY, 2 * FY), BF16),
                 pltpu.VMEM((2 * FX, 3 * NX), BF16),
+                pltpu.SemaphoreType.DMA((4,)),
                 pltpu.SemaphoreType.DMA((6,)),
                 pltpu.SemaphoreType.DMA((6,)),
+                pltpu.SemaphoreType.DMA((NF,)),
+                pltpu.SemaphoreType.DMA,
             ],
             compiler_params=pltpu.CompilerParams(
-                collective_id=0, has_side_effects=True, vmem_limit_bytes=40 * 1024 * 1024
+                collective_id=0, has_side_effects=True, vmem_limit_bytes=63 * 1024 * 1024
             ),
         )(
             source[0, :, 0], labels[0], speed_table, atten_table, offsets,

time: 102 us -> 87.5 us (0.86)
  Pallas kernels: 95.4 us -> 85.1 us
  local copies, waits for them, and re-layouts: 6.28 us -> 1.57 us
    pallas_call x1, Pallas kernels: 95.4 us -> 85.1 us  [local(): pl.pallas_call(kernel, out_shape=jax.ShapeDtypeStruct((TS // NF, 1, FX, F...]
    unnamed x19 -> x1, local copies, waits for them, and re-layouts: 6.28 us -> 1.57 us
where the time goes in v1:
time: 87.5 us; the launch traced here: 86.7 us
  Pallas kernels  85.1 us (97%)
  local copies, waits for them, and re-layouts  1.57 us (2%)
    pallas_call x1, Pallas kernels, local(): pl.pallas_call(kernel, out_shape=jax.ShapeDtypeStruct((TS // NF, 1, FX, F...  85.1 us

profile of v1, /device:TPU:1, one launch (start us, length us, event | category | flops | bytes accessed | tf_op | source)
XLA Modules:
  0.0 86.7 jit_solution(18308129113708657507)
XLA Ops:
  0.0 85.1 %shard_map.91 = f32[8,1,32,128]{3,2,1,0:T(8,128)} custom-call(f32[2,192,256]{2,1,0:T(8,128)} %bitcast.2, s32[192,256]{1,0:T(8,128)} %bitcast.3, f32[8]{0:T(128)} %speed.1, f32[8]{0:T(128)} %atten.1, s32[2]{0:T(128)} %offsets.1, bf16[768,512]{1,0:T(8,128)(2,1)} %constant.8.clone.table_y_in, bf16[384,576]{1,0:T(8,128)(2,1)} %constant.9.clone.table_x_in, ...), custom_call_target="tpu_custom_call" | custom-call | tf_op jit(solution)/shard_map/pallas_call | solution.py:483
  85.1 1.6 %copy.11 = f32[8,1,32,128]{3,2,1,0:T(8,128)} copy(f32[8,1,32,128]{3,2,1,0:T(8,128)} %shard_map.91) | data formatting | bytes 262144

commit v2 on v1

--- a/solution.py
+++ b/solution.py
@@ -12,6 +12,10 @@
 MESH = pl.DeviceIdType.MESH
 NX, NY, NZ = 192, 256, 64
 FX, FY, NF, TS, NMAT = 32, 128, 8, 64, 8
+LABELS, WINDOW = 8, 9
+BOTH, EACH = ((0, 12, 2),), ((0, 6, 2), (1, 6, 2))
+PARTS1, PARTS2, PARTS3 = BOTH, BOTH, BOTH
+HALF = 128
 BASE_BIN, K_UNIT = 4, 0.1
 F32, BF16 = jnp.float32, jnp.bfloat16
 
@@ -30,7 +34,9 @@
 
 def constant_tables():
     cos_y, sin_y = dft_tables(NY)
-    high, low = halves(np.concatenate([cos_y, sin_y], 1))
+    high, low = halves(
+        np.concatenate([cos_y[:, :HALF], sin_y[:, :HALF], cos_y[:, HALF:], sin_y[:, HALF:]], 1)
+    )
     table_y = np.concatenate([high, high, low], 0)
     cos_x, sin_x = dft_tables(NX)
     high, low = halves(np.concatenate([cos_x, sin_x], 0))
@@ -74,11 +80,11 @@
     return real, imag
 
 
-def along_y(real, imag, table, sign):
-    rows = real.shape[0]
-    return combine_rows(
-        times_table(jnp.concatenate([real, imag], 0), table), rows, NY, sign
-    )
+def along_y(real, imag, table, half, sign):
+    product = times_table(
+        jnp.concatenate([real, imag], 0), table[:, 2 * HALF * half : 2 * HALF * (half + 1)]
+    )
+    return combine_rows(product, NX, HALF, sign)
 
 
 def along_x(real, imag, table, sign):
@@ -95,48 +101,28 @@
     )
 
 
-def put_rows(ref, real, imag):
+def rows_of(half, i, part, per):
+    return pl.ds(6 * half + 2 * i + part, 64, stride=6 * per)
+
+
+def put_rows(ref, real, imag, half, per=2):
     for part, value in enumerate((real, imag)):
         for i in range(3):
-            for half in range(2):
-                ref[pl.ds(4 * i + 2 * part + half, 64, stride=12), :] = value[
-                    64 * i : 64 * i + 64, 128 * half : 128 * half + 128
-                ]
-
-
-def get_rows(ref, part, per):
-    return jnp.concatenate(
-        [
-            jnp.concatenate(
-                [
-                    ref[pl.ds(2 * per * i + per * part + half, 64, stride=6 * per), :]
-                    for half in range(per)
-                ],
-                1,
-            )
-            for i in range(3)
-        ],
-        0,
-    )
-
-
-def get_lines(ref, part):
-    return jnp.concatenate(
-        [
-            ref[pl.ds(4 * i + 2 * part + half, 64, stride=12), :]
-            for i in range(3)
-            for half in range(2)
-        ],
-        1,
-    )
-
-
-def put_lines(ref, real, imag):
+            ref[rows_of(half, i, part, per), :] = value[64 * i : 64 * i + 64]
+
+
+def get_rows(ref, part, half, per=2):
+    return jnp.concatenate([ref[rows_of(half, i, part, per), :] for i in range(3)], 0)
+
+
+def get_lines(ref, part, half):
+    return jnp.concatenate([ref[rows_of(half, i, part, 2), :] for i in range(3)], 1)
+
+
+def put_lines(ref, real, imag, half):
     for part, value in enumerate((real, imag)):
         for i in range(3):
-            for half in range(2):
-                at = 256 * i + 128 * half
-                ref[pl.ds(4 * i + 2 * part + half, 64, stride=12), :] = value[:, at : at + 128]
+            ref[rows_of(half, i, part, 2), :] = value[:, HALF * i : HALF * (i + 1)]
 
 
 def folded_square(index, count):
@@ -151,10 +137,10 @@
 
 
 def kernel(
-    source_in, labels, speed, atten, offsets, table_y_in, table_x_in, table_z_in, wave_table, out,
-    source, table_y, table_x, table_z,
+    source_in, labels, speed_in, atten_in, offsets_in, table_y_in, table_x_in, table_z_in, wave_in, out,
+    source, table_y, table_x, table_z, speed, atten, offsets, wave_table,
     send1, recv1, send2, recv2, send3, recv3, send4, recv4, tissue, window, windows,
-    green, spectrum, field_buf, sel_y, sel_x, load_sem, send_sem, recv_sem, pass_sem, relay_sem,
+    green, spectrum, field_buf, sel_y, sel_x, load_sem, send_sem, recv_sem, pass_sem, relay_sem, swap_sem,
 ):
     f = lax.axis_index("freq")
     s = lax.axis_index("slab")
@@ -166,7 +152,10 @@
     loads = [
         pltpu.make_async_copy(src, dst, load_sem.at[i])
         for i, (src, dst) in enumerate(
-            ((source_in, source), (table_y_in, table_y), (table_x_in, table_x), (table_z_in, table_z))
+            (
+                (source_in, source), (table_y_in, table_y), (table_x_in, table_x), (table_z_in, table_z),
+                (speed_in, speed), (atten_in, atten), (offsets_in, offsets), (wave_in, wave_table),
+            )
         )
     ]
     for load in loads:
@@ -194,23 +183,29 @@
             device_id_type=MESH,
         )
 
-    def exchange(src, dst, rows, sem):
+    def span(k, part):
+        first, rows, per = part
+        return pl.ds(6 * per * k + 6 * first, rows)
+
+    def exchange(src, dst, part, sem):
         def step(i, carry):
             k = lax.rem(mine + i, 64)
             remote(
-                src.at[pl.ds(rows * k, rows)],
-                dst.at[pl.ds(rows * mine, rows)],
-                sem,
-                role_device(freq, k),
+                src.at[span(k, part)], dst.at[span(mine, part)], sem, role_device(freq, k)
             ).start()
             return carry
 
         lax.fori_loop(1, 64, step, 0)
-        own = pl.ds(rows * mine, rows)
+        own = span(mine, part)
         pltpu.make_async_copy(src.at[own], dst.at[own], recv_sem.at[sem]).start()
 
     def arrived(ref, sem):
         pltpu.make_async_copy(ref, ref, recv_sem.at[sem]).wait()
+
+    def received(ref, parts, half, sem):
+        for first, rows, _ in parts:
+            if first == half:
+                arrived(ref.at[pl.ds(0, 64 * rows)], sem + first)
 
     def sent(ref, rows, sem):
         part = ref.at[pl.ds(0, rows)]
@@ -218,35 +213,50 @@
 
     loads[0].wait()
     loads[1].wait()
-    real, imag = along_y(source[0], source[1], table_y[...], -1.0)
     loads[2].wait()
-    real, imag = along_x(real, imag, table_x[...], -1.0)
-    put_rows(send1, real, imag)
+    for half in range(2):
+        real, imag = along_y(source[0], source[1], table_y, half, -1.0)
+        real, imag = along_x(real, imag, table_x[...], -1.0)
+        put_rows(send1, real, imag, half)
     pl.semaphore_wait(barrier, 64 + NF - 1)
 
-    def scatter(i, carry):
-        k = lax.rem(mine + i, 64)
-        remote(
-            send1.at[pl.ds(12 * k, 12)],
-            recv1.at[pl.ds(12 * s, 12)],
-            0,
-            role_device(f, k),
-        ).start()
-        return carry
-
-    lax.fori_loop(1, 64, scatter, 0)
-    own_send = send1.at[pl.ds(12 * mine, 12)]
-    own_recv = recv1.at[pl.ds(12 * s, 12)]
-
-    @pl.when(home)
-    def _():
-        pltpu.make_async_copy(own_send, own_recv, recv_sem.at[0]).start()
-
-    @pl.when(jnp.logical_not(home))
-    def _():
-        remote(own_send, own_recv, 0, role_device(f, mine)).start()
-
     stays = home & (mine == s)
+    first_rows = pl.ds(pl.multiple_of(96 * (f // 2 % 2), 8), 96)
+    role_rows = pl.ds(pl.multiple_of(96 * (freq // 2 % 2), 8), 96)
+    other_rows = pl.ds(pl.multiple_of(96 - 96 * (freq // 2 % 2), 8), 96)
+
+    early = (f // 2 + 4 * (f % 2) < 3)
+
+    @pl.when(early & stays)
+    def _():
+        pltpu.make_async_copy(labels.at[first_rows], tissue.at[first_rows], recv_sem.at[LABELS]).start()
+
+    @pl.when(early & jnp.logical_not(stays))
+    def _():
+        remote(labels.at[first_rows], tissue.at[first_rows], LABELS, role_device(f, s)).start()
+
+    for part in PARTS1:
+
+        def scatter(i, carry, part=part):
+            k = lax.rem(mine + i, 64)
+            remote(
+                send1.at[span(k, part)], recv1.at[span(s, part)], part[0], role_device(f, k)
+            ).start()
+            return carry
+
+        lax.fori_loop(1, 64, scatter, 0)
+        own_send, own_recv = send1.at[span(mine, part)], recv1.at[span(s, part)]
+
+        @pl.when(home)
+        def _(part=part, own_send=own_send, own_recv=own_recv):
+            pltpu.make_async_copy(own_send, own_recv, recv_sem.at[part[0]]).start()
+
+        @pl.when(jnp.logical_not(home))
+        def _(part=part, own_send=own_send, own_recv=own_recv):
+            remote(own_send, own_recv, part[0], role_device(f, mine)).start()
+
+    for load in loads[3:]:
+        load.wait()
 
     wave = K_UNIT * (BASE_BIN + freq).astype(F32)
     k0sq = wave * wave
@@ -263,16 +273,17 @@
     eps = jnp.sqrt(largest) + 0.1 * k0sq
     pot_imag = [value - eps for value in pot_imag]
     eps_row = eps[0:1, 0:1]
-    lines = (NZ, NY)
+    lines = (NZ, HALF)
     z_sq = folded_square(lax.broadcasted_iota(jnp.int32, lines, 0), NZ)
-    y_sq = folded_square(lax.broadcasted_iota(jnp.int32, lines, 1), NY)
-    for i in range(3):
-        x_sq = folded_square(jnp.full(lines, 64 * i + mine, jnp.int32), NX)
-        shifted = z_sq + x_sq + y_sq - k0sq
-        denom = shifted * shifted + eps_row * eps_row
-        weight = (1.0 / (NX * NY * NZ)) / denom
-        green[0, :, NY * i : NY * (i + 1)] = shifted * weight
-        green[1, :, NY * i : NY * (i + 1)] = eps_row * weight
+    for half in range(2):
+        y_sq = folded_square(lax.broadcasted_iota(jnp.int32, lines, 1) + HALF * half, NY)
+        for i in range(3):
+            x_sq = folded_square(jnp.full(lines, 64 * i + mine, jnp.int32), NX)
+            shifted = z_sq + x_sq + y_sq - k0sq
+            denom = shifted * shifted + eps_row * eps_row
+            weight = (1.0 / (NX * NY * NZ)) / denom
+            green[half, 0, :, HALF * i : HALF * (i + 1)] = shifted * weight
+            green[half, 1, :, HALF * i : HALF * (i + 1)] = eps_row * weight
 
     off_x, off_y = offsets[0], offsets[1]
     pick_y = (
@@ -285,36 +296,38 @@
     ).astype(F32).astype(BF16)
     for j, at in enumerate((0, 2 * NY)):
         for part in range(2):
-            piece = table_y[at : at + NY, NY * part : NY * (part + 1)]
+            piece = jnp.concatenate(
+                [
+                    table_y[at : at + NY, HALF * (2 * half + part) : HALF * (2 * half + part + 1)]
+                    for half in range(2)
+                ],
+                1,
+            )
             sel_y[NY * j : NY * (j + 1), FY * part : FY * (part + 1)] = dot(piece, pick_y).astype(BF16)
     for part in range(2):
         piece = table_x[NX * part : NX * (part + 1), :]
         sel_x[FX * part : FX * (part + 1), :] = dot(pick_x, piece).astype(BF16)
 
-    loads[3].wait()
-    @pl.when(home)
-    def _():
-        sent(send1, 12 * 63, 0)
-
-    @pl.when(jnp.logical_not(home))
-    def _():
-        sent(send1, 12 * 64, 0)
-
-    @pl.when(stays)
-    def _():
-        pltpu.make_async_copy(labels, tissue, recv_sem.at[1]).start()
-
-    @pl.when(jnp.logical_not(stays))
-    def _():
-        remote(labels, tissue, 1, role_device(f, s)).start()
-
-    arrived(recv1, 0)
-    real, imag = along_z(get_lines(recv1, 0), get_lines(recv1, 1), table_z[...], -1.0)
-    spectrum[0] = real
-    spectrum[1] = imag
-
-    def filtered(real, imag):
-        green_real, green_imag = green[0], green[1]
+    for first, rows, _ in PARTS1:
+
+        @pl.when(home)
+        def _(first=first, rows=rows):
+            sent(send1, rows * 63, first)
+
+        @pl.when(jnp.logical_not(home))
+        def _(first=first, rows=rows):
+            sent(send1, rows * 64, first)
+
+    @pl.when(jnp.logical_not(early) & stays)
+    def _():
+        pltpu.make_async_copy(labels.at[first_rows], tissue.at[first_rows], recv_sem.at[LABELS]).start()
+
+    @pl.when(jnp.logical_not(early) & jnp.logical_not(stays))
+    def _():
+        remote(labels.at[first_rows], tissue.at[first_rows], LABELS, role_device(f, s)).start()
+
+    def filtered(real, imag, half):
+        green_real, green_imag = green[half, 0], green[half, 1]
         return along_z(
             real * green_real - imag * green_imag,
             real * green_imag + imag * green_real,
@@ -322,14 +335,40 @@
             1.0,
         )
 
-    real, imag = filtered(real, imag)
-    put_lines(send2, real, imag)
-    exchange(send2, recv2, 12, 2)
-
-    arrived(recv2, 2)
-    real, imag = along_x(get_rows(recv2, 0, 2), get_rows(recv2, 1, 2), table_x[...], 1.0)
-    real, imag = along_y(real, imag, table_y[...], 1.0)
-    arrived(tissue, 1)
+    for half in range(2):
+        received(recv1, PARTS1, half, 0)
+        real, imag = along_z(
+            get_lines(recv1, 0, half), get_lines(recv1, 1, half), table_z[...], -1.0
+        )
+        spectrum[half, 0] = real
+        spectrum[half, 1] = imag
+        real, imag = filtered(real, imag, half)
+        put_lines(send2, real, imag, half)
+        if len(PARTS2) == 2:
+            exchange(send2, recv2, PARTS2[half], 2 + half)
+    if len(PARTS2) == 1:
+        exchange(send2, recv2, PARTS2[0], 2)
+
+    arrived(tissue.at[role_rows], LABELS)
+    swap = pltpu.make_async_remote_copy(
+        src_ref=tissue.at[role_rows],
+        dst_ref=tissue.at[role_rows],
+        send_sem=swap_sem.at[0],
+        recv_sem=swap_sem.at[1],
+        device_id=(f + 4 - 8 * (f // 4), s),
+        device_id_type=MESH,
+    )
+    swap.start()
+    pieces = []
+    for half in range(2):
+        received(recv2, PARTS2, half, 2)
+        pieces.append(
+            along_x(get_rows(recv2, 0, half), get_rows(recv2, 1, half), table_x[...], 1.0)
+        )
+    real, imag = (jnp.concatenate(pair, 1) for pair in zip(*pieces, strict=True))
+    pieces = [along_y(real, imag, table_y, half, 1.0) for half in range(2)]
+    real, imag = (jnp.concatenate(pair, 1) for pair in zip(*pieces, strict=True))
+    pltpu.make_async_copy(tissue.at[other_rows], tissue.at[other_rows], swap_sem.at[1]).wait()
     plane = (NX, NY)
     ids = tissue[...]
     cell_real = jnp.zeros(plane, F32)
@@ -346,10 +385,14 @@
     field_buf[1] = field_imag
     work_real = cell_real * field_real - cell_imag * field_imag
     work_imag = cell_real * field_imag + cell_imag * field_real
-    real, imag = along_y(work_real, work_imag, table_y[...], -1.0)
-    real, imag = along_x(real, imag, table_x[...], -1.0)
-    put_rows(send3, real, imag)
-    exchange(send3, recv3, 12, 3)
+    for half in range(2):
+        real, imag = along_y(work_real, work_imag, table_y, half, -1.0)
+        real, imag = along_x(real, imag, table_x[...], -1.0)
+        put_rows(send3, real, imag, half)
+        if len(PARTS3) == 2:
+            exchange(send3, recv3, PARTS3[half], 4 + half)
+    if len(PARTS3) == 1:
+        exchange(send3, recv3, PARTS3[0], 4)
 
     def focal(high_mid_low):
         total = None
@@ -374,24 +417,25 @@
         cell_imag = jnp.where(matched, pot_imag[m][0:1, 0:1], cell_imag)
     gamma_real, gamma_imag = -cell_imag * inv_eps, cell_real * inv_eps
 
-    arrived(recv3, 3)
-    real, imag = along_z(get_lines(recv3, 0), get_lines(recv3, 1), table_z[...], -1.0)
-    real, imag = filtered(real + spectrum[0], imag + spectrum[1])
-    stacked = jnp.concatenate(
-        [value[:, NY * i : NY * (i + 1)] for value in (real, imag) for i in range(3)], 0
-    )
-    high, low = split(stacked)
-    product = dot(jnp.concatenate([high, low], 1), jnp.concatenate([sel_y[:NY], sel_y[:NY]], 0)) + dot(
-        high, sel_y[NY:]
-    )
+    product = jnp.zeros((6 * NZ, 2 * FY), F32)
+    for half in range(2):
+        received(recv3, PARTS3, half, 4)
+        real, imag = along_z(
+            get_lines(recv3, 0, half), get_lines(recv3, 1, half), table_z[...], -1.0
+        )
+        real, imag = filtered(real + spectrum[half, 0], imag + spectrum[half, 1], half)
+        stacked = jnp.concatenate(
+            [value[:, HALF * i : HALF * (i + 1)] for value in (real, imag) for i in range(3)], 0
+        )
+        high = sel_y[HALF * half : HALF * (half + 1)]
+        low = sel_y[NY + HALF * half : NY + HALF * (half + 1)]
+        product = product + times_table(stacked, jnp.concatenate([high, high, low], 0))
     real, imag = combine_rows(product, 3 * NZ, FY, 1.0)
-    for part, value in enumerate((real, imag)):
-        for i in range(3):
-            send4[pl.ds(2 * i + part, 64, stride=6), :] = value[64 * i : 64 * i + 64]
-    exchange(send4, recv4, 6, 4)
-    arrived(recv4, 4)
+    put_rows(send4, real, imag, 0, 1)
+    exchange(send4, recv4, (0, 6, 1), 6)
+    arrived(recv4, 6)
     product = table_times(
-        sel_x[...], jnp.concatenate([get_rows(recv4, 0, 1), get_rows(recv4, 1, 1)], 1)
+        sel_x[...], jnp.concatenate([get_rows(recv4, 0, 0, 1), get_rows(recv4, 1, 0, 1)], 1)
     )
     real, imag = combine_tables(product, FX, FY, 1.0)
     diff_real = focal_real - real
@@ -405,7 +449,7 @@
         return pltpu.make_async_remote_copy(
             src_ref=window,
             dst_ref=windows.at[freq],
-            send_sem=send_sem.at[5],
+            send_sem=send_sem.at[WINDOW],
             recv_sem=pass_sem.at[freq],
             device_id=(target, mine),
             device_id_type=MESH,
@@ -451,21 +495,24 @@
 
     @pl.when(jnp.logical_not(stays))
     def _():
-        pltpu.make_async_copy(labels, labels, send_sem.at[1]).wait()
-
-    sent(send2, 12 * 63, 2)
-    sent(send3, 12 * 63, 3)
-    sent(send4, 6 * 63, 4)
+        pltpu.make_async_copy(tissue.at[first_rows], tissue.at[first_rows], send_sem.at[LABELS]).wait()
+
+    swap.wait_send()
+    for first, rows, _ in PARTS2:
+        sent(send2, rows * 63, 2 + first)
+    for first, rows, _ in PARTS3:
+        sent(send3, rows * 63, 4 + first)
+    sent(send4, 6 * 63, 6)
 
     @pl.when(at_home)
     def _():
         part = windows.at[pl.ds(0, 3)]
-        pltpu.make_async_copy(part, part, send_sem.at[5]).wait()
+        pltpu.make_async_copy(part, part, send_sem.at[WINDOW]).wait()
 
     @pl.when(jnp.logical_not(at_home))
     def _():
         part = windows.at[pl.ds(0, 4)]
-        pltpu.make_async_copy(part, part, send_sem.at[5]).wait()
+        pltpu.make_async_copy(part, part, send_sem.at[WINDOW]).wait()
 
     relayed = windows.at[pl.ds(0, 4)]
     pltpu.make_async_copy(relayed, relayed, relay_sem).wait()
@@ -475,7 +522,6 @@
     table_y, table_x, table_z, wave_table = constant_tables()
     vmem = pl.BlockSpec(memory_space=pltpu.VMEM)
     hbm = pl.BlockSpec(memory_space=pltpu.HBM)
-    smem = pl.BlockSpec(memory_space=pltpu.SMEM)
 
     def local(source, labels, speed_table, atten_table, offsets):
         chunks = pltpu.VMEM((64 * 12, 128), F32)
@@ -483,27 +529,32 @@
         return pl.pallas_call(
             kernel,
             out_shape=jax.ShapeDtypeStruct((TS // NF, 1, FX, FY), F32),
-            in_specs=[hbm, hbm, smem, smem, smem, hbm, hbm, hbm, smem],
+            in_specs=[hbm] * 9,
             out_specs=vmem,
             scratch_shapes=[
                 pltpu.VMEM((2, NX, NY), F32),
                 pltpu.VMEM(table_y.shape, BF16),
                 pltpu.VMEM(table_x.shape, BF16),
                 pltpu.VMEM(table_z.shape, BF16),
+                pltpu.SMEM((NMAT,), F32),
+                pltpu.SMEM((NMAT,), F32),
+                pltpu.SMEM((2,), jnp.int32),
+                pltpu.SMEM((2, TS), F32),
                 chunks, chunks, chunks, chunks, chunks, chunks, small, small,
                 pltpu.VMEM((NX, NY), jnp.int32),
                 pltpu.VMEM((2 * FX, FY), F32),
                 pltpu.VMEM((NF, 2 * FX, FY), F32),
-                pltpu.VMEM((2, NZ, 3 * NY), F32),
-                pltpu.VMEM((2, NZ, 3 * NY), F32),
+                pltpu.VMEM((2, 2, NZ, 3 * HALF), F32),
+                pltpu.VMEM((2, 2, NZ, 3 * HALF), F32),
                 pltpu.VMEM((2, NX, NY), F32),
                 pltpu.VMEM((2 * NY, 2 * FY), BF16),
                 pltpu.VMEM((2 * FX, 3 * NX), BF16),
-                pltpu.SemaphoreType.DMA((4,)),
-                pltpu.SemaphoreType.DMA((6,)),
-                pltpu.SemaphoreType.DMA((6,)),
+                pltpu.SemaphoreType.DMA((8,)),
+                pltpu.SemaphoreType.DMA((10,)),
+                pltpu.SemaphoreType.DMA((10,)),
                 pltpu.SemaphoreType.DMA((NF,)),
                 pltpu.SemaphoreType.DMA,
+                pltpu.SemaphoreType.DMA((2,)),
             ],
             compiler_params=pltpu.CompilerParams(
                 collective_id=0, has_side_effects=True, vmem_limit_bytes=63 * 1024 * 1024

time: 87.5 us -> 83.5 us (0.954)
  Pallas kernels: 85.1 us -> 81.8 us
    pallas_call x1, Pallas kernels: 85.1 us -> 81.8 us  [local(): pl.pallas_call(kernel, out_shape=jax.ShapeDtypeStruct((TS // NF, 1, FX, F...]
where the time goes in v2:
time: 83.5 us; the launch traced here: 83.4 us
  Pallas kernels  81.8 us (98%)
  local copies, waits for them, and re-layouts  1.57 us (2%)
    pallas_call x1, Pallas kernels, local(): pl.pallas_call(kernel, out_shape=jax.ShapeDtypeStruct((TS // NF, 1, FX, F...  81.8 us

profile of v2, /device:TPU:1, one launch (start us, length us, event | category | flops | bytes accessed | tf_op | source)
XLA Modules:
  0.0 83.4 jit_solution(11580223889823832629)
XLA Ops:
  0.0 81.8 %shard_map.91 = f32[8,1,32,128]{3,2,1,0:T(8,128)} custom-call(f32[2,192,256]{2,1,0:T(8,128)} %bitcast.2, s32[192,256]{1,0:T(8,128)} %bitcast.3, f32[8]{0:T(128)} %speed_in.1, f32[8]{0:T(128)} %atten_in.1, s32[2]{0:T(128)} %offsets_in.1, bf16[768,512]{1,0:T(8,128)(2,1)} %constant.8.clone.table_y_in, bf16[384,576]{1,0:T(8,128)(2,1)} %constant.9.clone.table_x_in, ...), custom_call_target="tpu_custom_call" | custom-call | tf_op jit(solution)/shard_map/pallas_call | solution.py:529
  81.8 1.6 %copy.11 = f32[8,1,32,128]{3,2,1,0:T(8,128)} copy(f32[8,1,32,128]{3,2,1,0:T(8,128)} %shard_map.91) | data formatting | bytes 262144

commit v3 on v2

--- a/solution.py
+++ b/solution.py
@@ -433,7 +433,7 @@
     real, imag = combine_rows(product, 3 * NZ, FY, 1.0)
     put_rows(send4, real, imag, 0, 1)
     exchange(send4, recv4, (0, 6, 1), 6)
-    arrived(recv4, 6)
+    arrived(recv4.at[pl.ds(0, 64 * 6)], 6)
     product = table_times(
         sel_x[...], jnp.concatenate([get_rows(recv4, 0, 0, 1), get_rows(recv4, 1, 0, 1)], 1)
     )
@@ -524,8 +524,8 @@
     hbm = pl.BlockSpec(memory_space=pltpu.HBM)
 
     def local(source, labels, speed_table, atten_table, offsets):
-        chunks = pltpu.VMEM((64 * 12, 128), F32)
-        small = pltpu.VMEM((64 * 6, 128), F32)
+        chunks = pltpu.VMEM((64 * 12 + 16, 128), F32)
+        small = pltpu.VMEM((64 * 6 + 8, 128), F32)
         return pl.pallas_call(
             kernel,
             out_shape=jax.ShapeDtypeStruct((TS // NF, 1, FX, FY), F32),

time: 83.5 us -> 83.6 us (level)
  no operation moved by 1% of the time
where the time goes in v3:
time: 83.6 us; the launch traced here: 83.4 us
  Pallas kernels  81.8 us (98%)
  local copies, waits for them, and re-layouts  1.57 us (2%)
    pallas_call x1, Pallas kernels, local(): pl.pallas_call(kernel, out_shape=jax.ShapeDtypeStruct((TS // NF, 1, FX, F...  81.8 us

profile of v3, /device:TPU:1, one launch (start us, length us, event | category | flops | bytes accessed | tf_op | source)
XLA Modules:
  0.0 83.4 jit_solution(5050420346720355947)
XLA Ops:
  0.0 81.8 %shard_map.91 = f32[8,1,32,128]{3,2,1,0:T(8,128)} custom-call(f32[2,192,256]{2,1,0:T(8,128)} %bitcast.2, s32[192,256]{1,0:T(8,128)} %bitcast.3, f32[8]{0:T(128)} %speed_in.1, f32[8]{0:T(128)} %atten_in.1, s32[2]{0:T(128)} %offsets_in.1, bf16[768,512]{1,0:T(8,128)(2,1)} %constant.8.clone.table_y_in, bf16[384,576]{1,0:T(8,128)(2,1)} %constant.9.clone.table_x_in, ...), custom_call_target="tpu_custom_call" | custom-call | tf_op jit(solution)/shard_map/pallas_call | solution.py:529
  81.8 1.6 %copy.11 = f32[8,1,32,128]{3,2,1,0:T(8,128)} copy(f32[8,1,32,128]{3,2,1,0:T(8,128)} %shard_map.91) | data formatting | bytes 262144
